TPU v7x, 32 devices: a whole 2x2x4 slice. The times are simulated.
32 devices in a mesh: groups: 2 (over y), heads: 8 (over z, x), width: 2 (over core).
Axes of the slice: x: 2, y: 2, z: 4, core: 2. Of those that a mesh axis runs over, the one named last changes fastest.
Arguments:
- tokens: bfloat16 [768, 16384], P(('groups', 'heads'), 'width'), parts along dimension 0, may hold values from -20 to 20
- norm_gain: bfloat16 [16384], P('width'), may hold values from 0.4 to 12
- w_query: bfloat16 [16384, 16384], P('width', 'heads'), may hold values from -0.046875 to 0.046875
- key_weight_matrix: bfloat16 [16384, 1024], P('width', 'heads'), may hold values from -0.046875 to 0.046875
- value_weight_matrix: bfloat16 [16384, 1024], P('width', 'heads'), may hold values from -0.046875 to 0.046875
- w_out: bfloat16 [16384, 16384], P('width', 'heads'), may hold values from -0.046875 to 0.046875
- prompt_len: int32 [4], P('groups'), parts along dimension 0, may hold values from 48 to 192
- prefix_len: int32 [4], P('groups'), parts along dimension 0, may hold values from 1 to 96
Outputs:
- block_out: bfloat16 [768, 16384], P(('groups', 'width'), 'heads'), parts along dimension 0
There are 2 independent parts, one for each index of `groups`. A program takes and returns all parts, laid end to end along the dimension named above; an argument that names none is the same for every part. Nothing has to cross between parts.
All inputs are finite; a program needn't handle non-finite values.
Results may differ from a plain program's by a relative error of at most 0.005.
The roundings to bfloat16 on the way count: a program that leaves them out, or rounds other values in their place, can miss the bound.
Values may be sent and summed in bfloat16 or wider, within the bound.
A program may use at most 320 MiB of HBM per device.

v0:
```python
import math

import jax
import jax.numpy as jnp
from jax import lax
from jax.sharding import PartitionSpec as P

MODEL_WIDTH = 16384
QUERY_HEADS = 128
KEY_VALUE_HEADS = 8
HEAD_WIDTH = 128
PROMPT_SLOTS = 192


def rope_angles(length, head_size):
    half_size = head_size // 2
    indices = jnp.arange(half_size, dtype=jnp.float32)
    frequency = jnp.exp(-(2.0 * indices / head_size) * math.log(500000.0))
    wavelength = 2.0 * math.pi / frequency
    smooth = (8192.0 / wavelength - 1.0) / 3.0
    blended = (1.0 - smooth) * frequency / 8.0 + smooth * frequency
    frequency = jnp.where(
        wavelength < 2048.0, frequency, jnp.where(wavelength > 8192.0, frequency / 8.0, blended)
    )
    positions = jnp.arange(length, dtype=jnp.float32)
    angles = positions[:, None] * frequency[None, :]
    return (jnp.cos(angles), jnp.sin(angles))


def rotate(vectors, cosine_table, sine_table):
    half_size = vectors.shape[-1] // 2
    leading = vectors[..., :half_size]
    trailing = vectors[..., half_size:]
    cosine_wide = cosine_table[:, None, :]
    sine_wide = sine_table[:, None, :]
    return jnp.concatenate(
        [
            leading * cosine_wide - trailing * sine_wide,
            trailing * cosine_wide + leading * sine_wide,
        ],
        axis=-1,
    )


def allowed_mask(length, prompt_length, prefix_length):
    query_slot = jnp.arange(length, dtype=jnp.int32)[:, None]
    key_slot = jnp.arange(length, dtype=jnp.int32)[None, :]
    return (key_slot < prompt_length) & ((key_slot <= query_slot) | (key_slot < prefix_length))


def per_device(
    tokens,
    norm_gain,
    w_query,
    key_weight_matrix,
    value_weight_matrix,
    w_out,
    prompt_len,
    prefix_len,
):
    head_count = lax.axis_size("heads")
    width_count = lax.axis_size("width")
    head_index = lax.axis_index("heads")
    width_index = lax.axis_index("width")
    widened = tokens.astype(jnp.float32)
    square_sums = lax.psum(jnp.sum(widened * widened, axis=1), "width")
    normed_inputs = (
        widened
        * lax.rsqrt(square_sums[:, None] / MODEL_WIDTH + 1e-05)
        * norm_gain.astype(jnp.float32)[None, :]
    ).astype(jnp.bfloat16)
    query_cols = w_query.shape[1]
    pair_cols = key_weight_matrix.shape[1]
    all_rows = tokens.shape[0] * head_count
    half_rows = all_rows // width_count
    whole_rows = lax.all_gather(normed_inputs, "heads", axis=0, tiled=True)
    summed = lax.psum_scatter(
        jnp.concatenate(
            [
                jnp.dot(whole_rows, w_query, preferred_element_type=jnp.float32),
                jnp.dot(whole_rows, key_weight_matrix, preferred_element_type=jnp.float32),
                jnp.dot(whole_rows, value_weight_matrix, preferred_element_type=jnp.float32),
            ],
            axis=1,
        ),
        "width",
        scatter_dimension=0,
        tiled=True,
    )
    query_sum = summed[:, :query_cols]
    key_part = summed[:, query_cols : query_cols + pair_cols].astype(jnp.bfloat16)
    value_part = summed[:, query_cols + pair_cols :].astype(jnp.bfloat16)
    projected_key_rows, projected_value_rows = (
        lax.all_gather(key_part, "heads", axis=1, tiled=True),
        lax.all_gather(value_part, "heads", axis=1, tiled=True),
    )
    local_heads = query_cols // HEAD_WIDTH
    heads_per_group = QUERY_HEADS // KEY_VALUE_HEADS
    heads_sharing_key = max(local_heads // heads_per_group, 1)
    leading_shared_slot = head_index * local_heads // heads_per_group
    prompts_in_group = half_rows // PROMPT_SLOTS
    cosine_table, sine_table = rope_angles(PROMPT_SLOTS, HEAD_WIDTH)
    queries = rotate(
        query_sum.reshape(prompts_in_group, PROMPT_SLOTS, local_heads, HEAD_WIDTH),
        cosine_table,
        sine_table,
    ).astype(jnp.bfloat16)
    key_grid = jnp.swapaxes(
        projected_key_rows.reshape(prompts_in_group, PROMPT_SLOTS, HEAD_WIDTH, KEY_VALUE_HEADS),
        2,
        3,
    )
    value_grid = jnp.swapaxes(
        projected_value_rows.reshape(prompts_in_group, PROMPT_SLOTS, HEAD_WIDTH, KEY_VALUE_HEADS),
        2,
        3,
    )
    key_heads = lax.dynamic_slice_in_dim(key_grid, leading_shared_slot, heads_sharing_key, 2)
    rotated_keys = rotate(key_heads.astype(jnp.float32), cosine_table, sine_table).astype(
        jnp.bfloat16
    )
    value_heads = lax.dynamic_slice_in_dim(value_grid, leading_shared_slot, heads_sharing_key, 2)
    lengths_here = lax.dynamic_slice_in_dim(
        prompt_len, width_index * prompts_in_group, prompts_in_group
    )
    prefixes_here = lax.dynamic_slice_in_dim(
        prefix_len, width_index * prompts_in_group, prompts_in_group
    )
    allowed = allowed_mask(PROMPT_SLOTS, lengths_here[:, None, None], prefixes_here[:, None, None])
    grouped_queries = queries.reshape(
        prompts_in_group,
        PROMPT_SLOTS,
        heads_sharing_key,
        local_heads // heads_sharing_key,
        HEAD_WIDTH,
    )
    scores = jnp.einsum(
        "bqngd,bknd->bngqk", grouped_queries, rotated_keys, preferred_element_type=jnp.float32
    ) / math.sqrt(HEAD_WIDTH)
    scores = jnp.where(allowed[:, None, None], scores, jnp.float32(-1e30))
    row_peak = jnp.max(scores, axis=-1, keepdims=True)
    raised = jnp.exp(scores - row_peak)
    probabilities = (raised / jnp.sum(raised, axis=-1, keepdims=True)).astype(jnp.bfloat16)
    mixture = jnp.einsum(
        "bngqk,bknd->bqngd", probabilities, value_heads, preferred_element_type=jnp.float32
    )
    attended = mixture.astype(jnp.bfloat16).reshape(half_rows, query_cols)
    every_head = lax.all_gather(attended, "heads", axis=1, tiled=True)
    return jnp.dot(
        every_head,
        lax.all_gather(w_out, "width", axis=0, tiled=True),
        preferred_element_type=jnp.float32,
    ).astype(jnp.bfloat16)


def solution(mesh):
    in_specs = (
        P(("groups", "heads"), "width"),
        P("width"),
        P("width", "heads"),
        P("width", "heads"),
        P("width", "heads"),
        P("width", "heads"),
        P("groups"),
        P("groups"),
    )
    out_specs = P(("groups", "width"), "heads")
    return jax.shard_map(
        per_device, mesh=mesh, in_specs=in_specs, out_specs=out_specs, check_vma=False
    )
```

profile of v0, /device:TPU:0, one launch (start us, length us, event | category | flops | bytes accessed | tf_op | source)
XLA Modules:
  0.0 446.8 jit_solution(14332276276895928136)
XLA Ops:
  6.5 0.9 convert_element_type.48
  7.4 1.4 fusion.2
  8.8 2.6 psum.7
  11.4 2.3 fusion.4
  13.7 0.0 all-gather.4.cloned.1.call-update
  13.7 0.0 reduce-scatter.2.cloned.1.call-start
  13.7 101.7 %all-gather.4.cloned.1.call-done = bf16[384,8192]{1,0:T(8,128)(2,1)} async-done(((bf16[48,8192]{1,0:T(8,128)(2,1)}), bf16[384,8192]{1,0:T(8,128)(2,1)}) %all-gather.4.cloned.1.call-update) | async-done | bytes 6291472 | tf_op jit(solution)/shard_map/all_gather | solution.py:76
  115.4 18.8 %fusion.36 = f32[384,2048]{1,0:T(8,128)S(1)} fusion(bf16[384,8192]{1,0:T(8,128)(2,1)} %all-gather.4.cloned.1.call-done, bf16[8192,2048]{1,0:T(8,128)(2,1)} %param.10), kind=kOutput, calls=%fused_computation.57 | convolution fusion | flops 12884901888 | bytes 42991616 | tf_op jit(solution)/shard_map/dot_general | solution.py:80
  134.3 0.0 copy-start.4
  134.3 4.7 %fusion.37 = f32[384,128]{1,0:T(8,128)S(1)} fusion(bf16[384,8192]{1,0:T(8,128)(2,1)} %all-gather.4.cloned.1.call-done, bf16[8192,128]{1,0:T(8,128)(2,1)S(1)} %copy-done), kind=kOutput, calls=%fused_computation.58 | convolution fusion | flops 805306368 | bytes 8585216 | tf_op jit(solution)/shard_map/dot_general | solution.py:81
  139.1 0.5 copy-done.4
  139.5 1.8 fusion.38
  141.3 2.0 pad_maximum_fusion
  143.4 0.0 reduce-scatter.2.cloned.1.call-update
  143.4 0.0 all-gather.6.cloned.1.call-start
  143.4 0.6 copy-done.7
  144.0 0.6 dynamic_slice.8
  144.6 0.6 dynamic_slice.9
  145.2 1.3 iota_compare_fusion.1
  146.5 0.1 fusion.21
  146.7 1.1 fusion.23
  147.7 5.4 %reduce-scatter.2.cloned.1.call-done = f32[192,2304]{1,0:T(8,128)} async-done(((f32[384,2304]{1,0:T(8,128)}), f32[192,2304]{1,0:T(8,128)}) %reduce-scatter.2.cloned.1.call-update) | async-done | bytes 1769488 | tf_op jit(solution)/shard_map/reduce_scatter | solution.py:77
  153.1 1.7 convert.21
  154.8 27.1 %all_gather.16 = bf16[192,1024]{1,0:T(8,128)(2,1)S(1)} all-gather(bf16[192,128]{1,0:T(8,128)(2,1)S(1)} %get-tuple-element.9), channel_id=1, replica_groups=mesh['groups'=2,'heads'=8,'width'=2] {'heads'}, dimensions={1}, use_global_device_ids=true | all-gather | bytes 442368 | tf_op jit(solution)/shard_map/all_gather | solution.py:95
  181.9 0.2 copy.17
  182.1 27.2 %all_gather.17 = bf16[192,1024]{1,0:T(8,128)(2,1)S(1)} all-gather(bf16[192,128]{1,0:T(8,128)(2,1)S(1)} %get-tuple-element.10), channel_id=1, replica_groups=mesh['groups'=2,'heads'=8,'width'=2] {'heads'}, dimensions={1}, use_global_device_ids=true | all-gather | bytes 442368 | tf_op jit(solution)/shard_map/all_gather | solution.py:94
  209.3 0.2 copy.19
  209.5 0.3 constant_dynamic-slice_fusion
  209.8 0.1 copy.28
  209.9 0.4 fusion.29
  210.4 0.2 slice_bitcast_fusion
  210.6 0.3 copy.31
  210.9 0.0 copy-start.5
  210.9 2.1 fusion.34
  213.0 0.1 copy.18
  213.2 2.9 fusion.14
  216.1 1.1 fusion.1
  217.1 0.7 fusion
  217.9 1.1 fusion.11
  219.0 0.5 copy.24
  219.5 1.1 copy.46
  220.6 0.0 all-gather.6.cloned.1.call-update
  220.6 0.0 all-gather.8.cloned.1.call-start
  220.7 0.5 all-gather.8.cloned.1.call-update
  221.2 96.4 %all-gather.6.cloned.1.call-done = bf16[192,16384]{1,0:T(8,128)(2,1)} async-done(((bf16[192,2048]{1,0:T(8,128)(2,1)}), bf16[192,16384]{1,0:T(8,128)(2,1)}) %all-gather.6.cloned.1.call-update) | async-done | bytes 6291472 | tf_op jit(solution)/shard_map/all_gather | solution.py:148
  317.6 94.8 %all-gather.8.cloned.1.call-done = bf16[16384,2048]{1,0:T(8,128)(2,1)} async-done(((bf16[8192,2048]{1,0:T(8,128)(2,1)}), bf16[16384,2048]{1,0:T(8,128)(2,1)}) %all-gather.8.cloned.1.call-update) | async-done | bytes 67108880 | tf_op jit(solution)/shard_map/all_gather | solution.py:151
  412.4 27.9 %convolution_convert_fusion = bf16[192,2048]{1,0:T(8,128)(2,1)} fusion(bf16[192,16384]{1,0:T(8,128)(2,1)} %all-gather.6.cloned.1.call-done, bf16[16384,2048]{1,0:T(8,128)(2,1)} %all-gather.8.cloned.1.call-done), kind=kOutput, calls=%fused_computation.5 | convolution fusion | flops 12885295104 | bytes 74186752 | tf_op jit(solution)/shard_map/dot_general | solution.py:149
  440.3 0.0 copy-done.1
  (18 shorter events, 0.1 us)
Async XLA Ops:
  6.5 127.8 %copy-start = (bf16[8192,128]{1,0:T(8,128)(2,1)S(1)}, bf16[8192,128]{1,0:T(8,128)(2,1)}, u32[]{:S(2)}) copy-start(bf16[8192,128]{1,0:T(8,128)(2,1)} %param.11) | copy-start | bytes 6291460
  6.5 108.9 %all-gather.4.cloned.1.call-start = ((), (), s32[]{:S(2)}) async-start(), calls=%async_computation.1 | async-start | bytes 7077888 | tf_op jit(solution)/shard_map/all_gather | solution.py:76
  13.7 139.4 %reduce-scatter.2.cloned.1.call-start = ((), (), s32[]{:S(2)}) async-start(), calls=%async_computation.2 | async-start | bytes 5308416 | tf_op jit(solution)/shard_map/reduce_scatter | solution.py:77
  134.3 4.7 %copy-start.2 = (bf16[384,8192]{1,0:T(8,128)(2,1)S(1)}, bf16[384,8192]{1,0:T(8,128)(2,1)}, u32[]{:S(2)}) copy-start(bf16[384,8192]{1,0:T(8,128)(2,1)} %all-gather.4.cloned.1.call-done) | copy-start | bytes 18874372
  134.3 5.2 %copy-start.4 = (bf16[8192,128]{1,0:T(8,128)(2,1)S(1)}, bf16[8192,128]{1,0:T(8,128)(2,1)}, u32[]{:S(2)}) copy-start(bf16[8192,128]{1,0:T(8,128)(2,1)} %param.12) | copy-start | bytes 6291460
  143.4 0.7 copy-start.7
  143.4 1.3 copy-start.8
  143.4 174.2 %all-gather.6.cloned.1.call-start = ((), (), s32[]{:S(2)}) async-start(), calls=%async_computation.3 | async-start | bytes 7077888 | tf_op jit(solution)/shard_map/all_gather | solution.py:148
  153.1 57.3 %copy-start.3 = (f32[192,2304]{1,0:T(8,128)S(1)}, f32[192,2304]{1,0:T(8,128)}, u32[]{:S(2)}) copy-start(f32[192,2304]{1,0:T(8,128)} %reduce-scatter.2.cloned.1.call-done) | copy-start | bytes 5308420
  210.9 2.3 copy-start.5
  210.9 2.3 copy-start.6
  220.6 191.7 %all-gather.8.cloned.1.call-start = ((), (), s32[]{:S(2)}) async-start(), calls=%async_computation.4 | async-start | bytes 100663296 | tf_op jit(solution)/shard_map/all_gather | solution.py:151
  412.4 27.9 %copy-start.1 = (bf16[8192,128]{1,0:T(8,128)(2,1)S(1)}, bf16[8192,128]{1,0:T(8,128)(2,1)}, u32[]{:S(2)}) copy-start(bf16[8192,128]{1,0:T(8,128)(2,1)} %param.11) | copy-start | bytes 6291460
Sparse Core Ops, SparseCore 0:
  13.8 101.5 all-gather.3
  143.5 9.5 reduce-scatter.1
  220.7 96.7 all-gather.5
  319.0 93.2 all-gather.7
where the time goes:
time: 447 us
  waiting for transfers between devices  299 us (67%)
  blocking collectives  56.9 us (13%)
  matrix products  55.4 us (12%)
  other arithmetic  14.8 us (3%)
  between operations  13.3 us (3%)
  local copies, waits for them, and re-layouts  7.44 us (2%)
    all_gather x1, waiting for transfers between devices, per_device(): whole_rows = lax.all_gather(normed_inputs, 'heads', axis=0, tiled=True)  102 us
    all_gather x1, waiting for transfers between devices, per_device(): every_head = lax.all_gather(attended, 'heads', axis=1, tiled=True)  96.4 us
    all_gather x1, waiting for transfers between devices, per_device(): lax.all_gather(w_out, 'width', axis=0, tiled=True)  94.8 us
    dot_general x1, matrix products, per_device(): jnp.dot(every_head, lax.all_gather(w_out, 'width', axis=0, tiled=True), p...  27.9 us
    all_gather x1, blocking collectives, per_device(): lax.all_gather(key_part, 'heads', axis=1, tiled=True)  27.2 us
    all_gather x1, blocking collectives, per_device(): lax.all_gather(value_part, 'heads', axis=1, tiled=True)  27.1 us
    dot_general x1, matrix products, per_device(): jnp.dot(whole_rows, w_query, preferred_element_type=jnp.float32)  18.8 us
  transfers between devices with their start and end apart: 4, of which 4 were waited for; matrix products, arithmetic and copies ran while one was open for 1% of the time, Pallas kernels for 0%

commit v1 on v0

--- a/solution.py
+++ b/solution.py
@@ -74,10 +74,11 @@
     all_rows = tokens.shape[0] * head_count
     half_rows = all_rows // width_count
     whole_rows = lax.all_gather(normed_inputs, "heads", axis=0, tiled=True)
-    summed = lax.psum_scatter(
+    swap = [(i, (i + 1) % width_count) for i in range(width_count)]
+    other_rows = lax.ppermute(w_out, "width", swap)
+    pair_sum = lax.psum_scatter(
         jnp.concatenate(
             [
-                jnp.dot(whole_rows, w_query, preferred_element_type=jnp.float32),
                 jnp.dot(whole_rows, key_weight_matrix, preferred_element_type=jnp.float32),
                 jnp.dot(whole_rows, value_weight_matrix, preferred_element_type=jnp.float32),
             ],
@@ -86,13 +87,16 @@
         "width",
         scatter_dimension=0,
         tiled=True,
-    )
-    query_sum = summed[:, :query_cols]
-    key_part = summed[:, query_cols : query_cols + pair_cols].astype(jnp.bfloat16)
-    value_part = summed[:, query_cols + pair_cols :].astype(jnp.bfloat16)
-    projected_key_rows, projected_value_rows = (
-        lax.all_gather(key_part, "heads", axis=1, tiled=True),
-        lax.all_gather(value_part, "heads", axis=1, tiled=True),
+    ).astype(jnp.bfloat16)
+    pair_rows = lax.all_gather(pair_sum, "heads", axis=0, tiled=False)
+    pair_rows = pair_rows.reshape(head_count, half_rows, 2, pair_cols)
+    projected_key_rows = jnp.swapaxes(pair_rows[:, :, 0], 0, 1).reshape(half_rows, -1)
+    projected_value_rows = jnp.swapaxes(pair_rows[:, :, 1], 0, 1).reshape(half_rows, -1)
+    query_sum = lax.psum_scatter(
+        jnp.dot(whole_rows, w_query, preferred_element_type=jnp.float32),
+        "width",
+        scatter_dimension=0,
+        tiled=True,
     )
     local_heads = query_cols // HEAD_WIDTH
     heads_per_group = QUERY_HEADS // KEY_VALUE_HEADS
@@ -146,10 +150,13 @@
     )
     attended = mixture.astype(jnp.bfloat16).reshape(half_rows, query_cols)
     every_head = lax.all_gather(attended, "heads", axis=1, tiled=True)
-    return jnp.dot(
-        every_head,
-        lax.all_gather(w_out, "width", axis=0, tiled=True),
-        preferred_element_type=jnp.float32,
+    share = w_out.shape[0]
+    own_part = lax.dynamic_slice_in_dim(every_head, width_index * share, share, 1)
+    other_index = (width_index + 1) % width_count
+    other_part = lax.dynamic_slice_in_dim(every_head, other_index * share, share, 1)
+    return (
+        jnp.dot(own_part, w_out, preferred_element_type=jnp.float32)
+        + jnp.dot(other_part, other_rows, preferred_element_type=jnp.float32)
     ).astype(jnp.bfloat16)
 
 

time: 447 us -> 332 us (0.74)
  waiting for transfers between devices: 299 us -> 198 us
  blocking collectives: 56.9 us -> 34.9 us
  matrix products: 55.4 us -> 63.3 us
  other arithmetic: 14.8 us -> 9.58 us
    all_gather x1 -> x0, waiting for transfers between devices: 94.8 us -> none  [per_device(): lax.all_gather(w_out, 'width', axis=0, tiled=True)]
    all_gather x2 -> x1, blocking collectives: 54.3 us -> 32.3 us  [per_device(): pair_rows = lax.all_gather(pair_sum, 'heads', axis=0, tiled=False)]
    reduce_scatter x1 -> x2, waiting for transfers between devices: 5.38 us -> 0.04 us  [the longest x1 0.02 us: per_device(): lax.psum_scatter(jnp.concatenate([jnp.dot(whole_rows, key_weight_matrix,...]
    dot_general x1 -> x2, matrix products: 27.9 us -> 32.1 us  [the longest x1 16.2 us: per_device(): jnp.dot(own_part, w_out, preferred_element_type=jnp.float32)]
  transfers between devices with their start and end apart: 4 -> 5, of which waited for: 4 -> 2; matrix products, arithmetic and copies ran while one was open for 1% -> 19% of each run, Pallas kernels for 0% -> 0%
where the time goes in v1:
time: 332 us
  waiting for transfers between devices  198 us (60%)
  matrix products  63.3 us (19%)
  blocking collectives  34.9 us (11%)
  between operations  13.3 us (4%)
  local copies, waits for them, and re-layouts  11.5 us (3%)
  other arithmetic  9.58 us (3%)
    all_gather x1, waiting for transfers between devices, per_device(): whole_rows = lax.all_gather(normed_inputs, 'heads', axis=0, tiled=True)  101 us
    all_gather x1, waiting for transfers between devices, per_device(): every_head = lax.all_gather(attended, 'heads', axis=1, tiled=True)  97 us
    all_gather x1, blocking collectives, per_device(): pair_rows = lax.all_gather(pair_sum, 'heads', axis=0, tiled=False)  32.3 us
    dot_general x1, matrix products, per_device(): jnp.dot(whole_rows, w_query, preferred_element_type=jnp.float32)  22.3 us
    dot_general x1, matrix products, per_device(): jnp.dot(own_part, w_out, preferred_element_type=jnp.float32)  16.2 us
    dot_general x1, matrix products, per_device(): jnp.dot(other_part, other_rows, preferred_element_type=jnp.float32)  15.9 us
  transfers between devices with their start and end apart: 5, of which 2 were waited for; matrix products, arithmetic and copies ran while one was open for 19% of the time, Pallas kernels for 0%

profile of v1, /device:TPU:0, one launch (start us, length us, event | category | flops | bytes accessed | tf_op | source)
XLA Modules:
  0.0 331.6 jit_solution(7338332719740524649)
XLA Ops:
  6.5 1.5 fusion.12
  8.1 2.6 psum.7
  10.7 0.7 convert_element_type.49
  11.4 2.3 fusion.14
  13.7 0.0 all-gather.4.cloned.1.call-update
  13.7 0.0 reduce-scatter.7.cloned.1.call-start
  13.7 0.4 collective-permute-start
  14.1 101.3 %all-gather.4.cloned.1.call-done = bf16[384,8192]{1,0:T(8,128)(2,1)} async-done(((bf16[48,8192]{1,0:T(8,128)(2,1)}), bf16[384,8192]{1,0:T(8,128)(2,1)}) %all-gather.4.cloned.1.call-update) | async-done | bytes 6291472 | tf_op jit(solution)/shard_map/all_gather | solution.py:76
  115.4 4.8 %fusion.49 = f32[384,128]{0,1:T(8,128)S(1)} fusion(bf16[384,8192]{1,0:T(8,128)(2,1)} %all-gather.4.cloned.1.call-done, bf16[8192,128]{1,0:T(8,128)(2,1)S(1)} %copy-done), kind=kOutput, calls=%fused_computation.64 | convolution fusion | flops 805306368 | bytes 8585216 | tf_op jit(solution)/shard_map/dot_general | solution.py:83
  120.2 0.4 copy-done.3
  120.7 1.9 fusion.48
  122.6 0.9 copy.49
  123.5 0.0 reduce-scatter.7.cloned.1.call-update
  123.5 0.0 reduce-scatter.5.cloned.1.call-start
  123.6 22.3 %fusion.50 = f32[384,2048]{1,0:T(8,128)} fusion(bf16[384,8192]{1,0:T(8,128)(2,1)} %all-gather.4.cloned.1.call-done, bf16[8192,2048]{1,0:T(8,128)(2,1)} %param.10), kind=kOutput, calls=%fused_computation.65 | convolution fusion | flops 12884901888 | bytes 42991616 | tf_op jit(solution)/shard_map/dot_general | solution.py:96
  145.9 0.0 reduce-scatter.5.cloned.1.call-update
  145.9 0.0 all-gather.6.cloned.1.call-start
  146.0 0.6 copy-done.5
  146.5 0.6 dynamic_slice.15
  147.2 0.6 dynamic_slice.14
  147.8 1.3 iota_compare_fusion.1
  149.1 0.1 fusion.31
  149.3 0.4 fusion.33
  149.6 0.0 reduce-scatter.7.cloned.1.call-done
  149.7 1.0 convert_element_type.51
  150.7 32.3 %all-gather = bf16[1536,256]{1,0:T(8,128)(2,1)S(1)} all-gather(bf16[192,256]{1,0:T(8,128)(2,1)S(1)} %convert_element_type.51), channel_id=2, replica_groups=mesh['groups'=2,'heads'=8,'width'=2] {'heads'}, dimensions={0}, use_global_device_ids=true | all-gather | bytes 884736 | tf_op jit(solution)/shard_map/all_gather | solution.py:91
  183.0 0.2 reshape.260
  183.2 1.4 fusion.47
  184.6 1.2 copy.57
  185.9 1.2 copy.56
  187.1 0.3 constant_dynamic-slice_fusion
  187.4 0.1 copy.53
  187.5 0.1 copy.41
  187.7 0.4 fusion.39
  188.1 0.0 reduce-scatter.5.cloned.1.call-done
  188.1 1.7 copy.58
  189.8 0.5 fusion.46
  190.3 1.0 fusion.24
  191.3 1.0 fusion.11
  192.4 0.7 fusion.4
  193.1 1.1 fusion.21
  194.3 0.5 copy.47
  194.8 1.1 copy.73
  195.9 0.0 all-gather.6.cloned.1.call-update
  195.9 97.0 %all-gather.6.cloned.1.call-done = bf16[192,16384]{1,0:T(8,128)(2,1)} async-done(((bf16[192,2048]{1,0:T(8,128)(2,1)}), bf16[192,16384]{1,0:T(8,128)(2,1)}) %all-gather.6.cloned.1.call-update) | async-done | bytes 6291472 | tf_op jit(solution)/shard_map/all_gather | solution.py:152
  292.9 16.2 %fusion.2 = f32[192,2048]{1,0:T(8,128)} fusion(bf16[8192,2048]{1,0:T(8,128)(2,1)} %param.13, bf16[192,16384]{1,0:T(8,128)(2,1)} %all-gather.6.cloned.1.call-done, s32[]{:T(128)S(6)} %select_n.78), kind=kOutput, calls=%fused_computation.3 | convolution fusion | flops 6442450944 | bytes 38273028 | tf_op jit(solution)/shard_map/dot_general | solution.py:158
  309.2 0.0 collective-permute-done
  309.2 15.9 %fusion.8 = bf16[192,2048]{1,0:T(8,128)(2,1)} fusion(f32[192,2048]{1,0:T(8,128)} %fusion.2, bf16[8192,2048]{1,0:T(8,128)(2,1)} %collective-permute-done, bf16[192,16384]{1,0:T(8,128)(2,1)S(1)} %copy-done.4, s32[]{:T(128)S(6)} %select_n.80), kind=kOutput, calls=%fused_computation.9 | convolution fusion | flops 6443237376 | bytes 39059460 | tf_op jit(solution)/shard_map/dot_general | solution.py:159
  (17 shorter events, 0.1 us)
Async XLA Ops:
  6.5 108.9 %copy-start = (bf16[8192,128]{1,0:T(8,128)(2,1)S(1)}, bf16[8192,128]{1,0:T(8,128)(2,1)}, u32[]{:S(2)}) copy-start(bf16[8192,128]{1,0:T(8,128)(2,1)} %param.12) | copy-start | bytes 6291460
  6.5 108.9 %all-gather.4.cloned.1.call-start = ((), (), s32[]{:S(2)}) async-start(), calls=%async_computation.2 | async-start | bytes 7077888 | tf_op jit(solution)/shard_map/all_gather | solution.py:76
  13.7 136.0 %reduce-scatter.7.cloned.1.call-start = ((), (), s32[]{:S(2)}) async-start(), calls=%async_computation.5 | async-start | bytes 589824 | tf_op jit(solution)/shard_map/reduce_scatter | solution.py:79
  13.7 295.4 %collective-permute-start = (bf16[8192,2048]{1,0:T(8,128)(2,1)}, bf16[8192,2048]{1,0:T(8,128)(2,1)}, u32[]{:S(2)}, u32[]{:S(2)}) collective-permute-start(bf16[8192,2048]{1,0:T(8,128)(2,1)} %param.13), channel_id=1, source_target_pairs={{0,1},{1,0},{2,3},{3,2},{4,5},{5,4},{6,7},{7,6},{8,9},{9,8},{10,11... | collective-permute-start | bytes 100663304 | tf_op jit(solution)/shard_map/ppermute | solution.py:78
  115.4 4.8 %copy-start.2 = (bf16[384,8192]{1,0:T(8,128)(2,1)S(1)}, bf16[384,8192]{1,0:T(8,128)(2,1)}, u32[]{:S(2)}) copy-start(bf16[384,8192]{1,0:T(8,128)(2,1)} %all-gather.4.cloned.1.call-done) | copy-start | bytes 18874372
  115.4 5.2 %copy-start.3 = (bf16[8192,128]{1,0:T(8,128)(2,1)S(1)}, bf16[8192,128]{1,0:T(8,128)(2,1)}, u32[]{:S(2)}) copy-start(bf16[8192,128]{1,0:T(8,128)(2,1)} %param.11) | copy-start | bytes 6291460
  123.5 64.6 %reduce-scatter.5.cloned.1.call-start = ((), (), s32[]{:S(2)}) async-start(), calls=%async_computation.3 | async-start | bytes 4718592 | tf_op jit(solution)/shard_map/reduce_scatter | solution.py:95
  145.9 0.7 copy-start.5
  145.9 1.3 copy-start.6
  145.9 147.0 %all-gather.6.cloned.1.call-start = ((), (), s32[]{:S(2)}) async-start(), calls=%async_computation.4 | async-start | bytes 7077888 | tf_op jit(solution)/shard_map/all_gather | solution.py:152
  292.9 16.2 %copy-start.4 = (bf16[192,16384]{1,0:T(8,128)(2,1)S(1)}, bf16[192,16384]{1,0:T(8,128)(2,1)}, u32[]{:S(2)}) copy-start(bf16[192,16384]{1,0:T(8,128)(2,1)} %all-gather.6.cloned.1.call-done) | copy-start | bytes 18874372
  309.2 15.9 %copy-start.1 = (bf16[8192,128]{1,0:T(8,128)(2,1)S(1)}, bf16[8192,128]{1,0:T(8,128)(2,1)}, u32[]{:S(2)}) copy-start(bf16[8192,128]{1,0:T(8,128)(2,1)} %param.12) | copy-start | bytes 6291460
Sparse Core Ops, SparseCore 0:
  13.8 101.5 all-gather.3
  123.6 5.9 reduce-scatter.6
  146.0 9.0 reduce-scatter.4
  196.0 96.8 all-gather.5

commit v2 on v1

--- a/solution.py
+++ b/solution.py
@@ -1,8 +1,11 @@
+import functools
 import math
 
 import jax
 import jax.numpy as jnp
 from jax import lax
+from jax.experimental import pallas as pl
+from jax.experimental.pallas import tpu as pltpu
 from jax.sharding import PartitionSpec as P
 
 MODEL_WIDTH = 16384
@@ -46,6 +49,230 @@
     query_slot = jnp.arange(length, dtype=jnp.int32)[:, None]
     key_slot = jnp.arange(length, dtype=jnp.int32)[None, :]
     return (key_slot < prompt_length) & ((key_slot <= query_slot) | (key_slot < prefix_length))
+
+
+LAYERS = 4
+RING_SIZE = 8
+ARRIVAL = ((0, 1, 2, 3), (1, 0, 2, 3), (2, 3, 1, 0), (3, 2, 1, 0))
+SEQUENCE = ((0, 0), (1, 0), (0, 1), (2, 0), (1, 1), (3, 0), (2, 1), (3, 1))
+
+
+def layer_at(layer, place):
+    found = jnp.int32(ARRIVAL[LAYERS - 1][place])
+    for at in range(LAYERS - 1):
+        found = jnp.where(layer == at, ARRIVAL[at][place], found)
+    return found
+
+
+def enter(me):
+    layer, side = me // 2, me % 2
+    barrier = pltpu.get_barrier_semaphore()
+
+    def greet(target):
+        pl.semaphore_signal(
+            barrier, inc=1, device_id={"heads": target}, device_id_type=pl.DeviceIdType.MESH
+        )
+
+    greet(layer * 2 + 1 - side)
+
+    @pl.when(layer < LAYERS - 1)
+    def _():
+        greet(me + 2)
+
+    @pl.when(layer > 0)
+    def _():
+        greet(me - 2)
+
+    pl.semaphore_wait(
+        barrier,
+        1 + jnp.where(layer < LAYERS - 1, 1, 0) + jnp.where(layer > 0, 1, 0),
+    )
+
+
+def copies(me, place, chunk, view, send_sem, recv_sem):
+    layer, side = me // 2, me % 2
+    block_layer = layer_at(layer, place)
+    owner = block_layer * 2 + side
+    ref = view(owner, chunk)
+
+    def to(target, way):
+        return pltpu.make_async_remote_copy(
+            src_ref=ref,
+            dst_ref=ref,
+            send_sem=send_sem.at[way, place, chunk],
+            recv_sem=recv_sem.at[owner, chunk],
+            device_id={"heads": target},
+            device_id_type=pl.DeviceIdType.MESH,
+        )
+
+    return (
+        (to(me + 2, 0), jnp.logical_and(block_layer <= layer, layer < LAYERS - 1)),
+        (to(me - 2, 1), jnp.logical_and(block_layer >= layer, layer > 0)),
+        (to(layer * 2 + 1 - side, 2), None),
+    )
+
+
+def pass_on(me, place, chunk, view, send_sem, recv_sem):
+    for copy, holds in copies(me, place, chunk, view, send_sem, recv_sem):
+        if holds is None:
+            copy.start()
+        else:
+            pl.when(holds)(copy.start)
+
+
+def finish(me, chunks, view, send_sem, recv_sem):
+    for place in range(LAYERS):
+        for chunk in range(chunks):
+            for copy, holds in copies(me, place, chunk, view, send_sem, recv_sem):
+                if holds is None:
+                    copy.wait_send()
+                else:
+                    pl.when(holds)(copy.wait_send)
+
+
+def receive(me, step, chunks, view, send_sem, recv_sem):
+    layer, side = me // 2, me % 2
+    place, other = SEQUENCE[step]
+    owner = layer_at(layer, place) * 2 + (1 - side if other else side)
+    for chunk in range(chunks):
+        if step:
+            ref = view(owner, chunk)
+            pltpu.make_async_remote_copy(
+                src_ref=ref,
+                dst_ref=ref,
+                send_sem=send_sem.at[2, place, chunk],
+                recv_sem=recv_sem.at[owner, chunk],
+                device_id={"heads": layer * 2 + 1 - side},
+                device_id_type=pl.DeviceIdType.MESH,
+            ).wait_recv()
+        if not other:
+            pass_on(me, place, chunk, view, send_sem, recv_sem)
+    return owner
+
+
+def gather_kernel(chunks, own_ref, all_ref, own_sem, send_sem, recv_sem):
+    me = lax.axis_index("heads")
+    rows, cols = own_ref.shape
+    wide = cols // chunks
+
+    def view(owner, chunk):
+        return all_ref.at[pl.ds(pl.multiple_of(owner * rows, rows), rows), pl.ds(chunk * wide, wide)]
+
+    keep = pltpu.make_async_copy(
+        own_ref, all_ref.at[pl.ds(pl.multiple_of(me * rows, rows), rows)], own_sem
+    )
+    keep.start()
+    enter(me)
+    keep.wait()
+    for step in range(RING_SIZE):
+        receive(me, step, chunks, view, send_sem, recv_sem)
+    finish(me, chunks, view, send_sem, recv_sem)
+
+
+def gather_rows(block, chunks, collective_id):
+    rows, cols = block.shape
+    return pl.pallas_call(
+        functools.partial(gather_kernel, chunks),
+        out_shape=jax.ShapeDtypeStruct((rows * RING_SIZE, cols), block.dtype),
+        in_specs=[pl.BlockSpec(memory_space=pltpu.VMEM)],
+        out_specs=pl.BlockSpec(memory_space=pltpu.VMEM),
+        scratch_shapes=[
+            pltpu.SemaphoreType.DMA,
+            pltpu.SemaphoreType.DMA((3, LAYERS, chunks)),
+            pltpu.SemaphoreType.DMA((RING_SIZE, chunks)),
+        ],
+        compiler_params=pltpu.CompilerParams(
+            collective_id=collective_id, has_side_effects=True, vmem_limit_bytes=24 * 2**20
+        ),
+    )(block)
+
+
+WEIGHT_SLOTS = 3
+
+
+def project_kernel(
+    chunks, own_ref, near_ref, far_ref, out_ref,
+    held, total, weights, weight_sem, send_sem, recv_sem,
+):
+    me = lax.axis_index("heads")
+    core = lax.axis_index("width")
+    layer, side = me // 2, me % 2
+    rows, cols = own_ref.shape
+    wide = cols // chunks
+    per_half = near_ref.shape[0] // cols
+    tile = 256
+
+    def view(owner, chunk):
+        return held.at[owner, :, pl.ds(chunk * wide, wide)]
+
+    def fetch(step):
+        place, other = SEQUENCE[step]
+        owner = layer_at(layer, place) * 2 + (1 - side if other else side)
+        at = pl.ds(pl.multiple_of((owner % per_half) * cols, cols), cols)
+        slot = step % WEIGHT_SLOTS
+        near = owner // per_half == core
+
+        @pl.when(near)
+        def _():
+            pltpu.make_async_copy(near_ref.at[at], weights.at[slot], weight_sem.at[slot]).start()
+
+        @pl.when(jnp.logical_not(near))
+        def _():
+            pltpu.make_async_copy(far_ref.at[at], weights.at[slot], weight_sem.at[slot]).start()
+
+    for step in range(WEIGHT_SLOTS):
+        fetch(step)
+    held[me] = own_ref[...]
+    enter(me)
+    for step in range(RING_SIZE):
+        owner = receive(me, step, chunks, view, send_sem, recv_sem)
+        slot = step % WEIGHT_SLOTS
+        pltpu.make_async_copy(
+            near_ref.at[pl.ds(0, cols)], weights.at[slot], weight_sem.at[slot]
+        ).wait()
+
+        @pl.loop(0, out_ref.shape[1] // tile)
+        def _(n):
+            at = pl.ds(pl.multiple_of(n * tile, tile), tile)
+            term = jnp.dot(
+                held[owner], weights[slot, :, at], preferred_element_type=jnp.float32
+            )
+            if step == 0:
+                total[:, at] = term
+            elif step < RING_SIZE - 1:
+                total[:, at] += term
+            else:
+                out_ref[:, at] = (total[:, at] + term).astype(out_ref.dtype)
+
+        if step + WEIGHT_SLOTS < RING_SIZE:
+            fetch(step + WEIGHT_SLOTS)
+    finish(me, chunks, view, send_sem, recv_sem)
+
+
+def gather_and_project(block, near, far, chunks, collective_id):
+    rows, cols = block.shape
+    out_cols = near.shape[1]
+    return pl.pallas_call(
+        functools.partial(project_kernel, chunks),
+        out_shape=jax.ShapeDtypeStruct((rows, out_cols), jnp.bfloat16),
+        in_specs=[
+            pl.BlockSpec(memory_space=pltpu.VMEM),
+            pl.BlockSpec(memory_space=pl.ANY),
+            pl.BlockSpec(memory_space=pl.ANY),
+        ],
+        out_specs=pl.BlockSpec(memory_space=pltpu.VMEM),
+        scratch_shapes=[
+            pltpu.VMEM((RING_SIZE, rows, cols), block.dtype),
+            pltpu.VMEM((rows, out_cols), jnp.float32),
+            pltpu.VMEM((WEIGHT_SLOTS, cols, out_cols), near.dtype),
+            pltpu.SemaphoreType.DMA((WEIGHT_SLOTS,)),
+            pltpu.SemaphoreType.DMA((3, LAYERS, chunks)),
+            pltpu.SemaphoreType.DMA((RING_SIZE, chunks)),
+        ],
+        compiler_params=pltpu.CompilerParams(
+            collective_id=collective_id, has_side_effects=True, vmem_limit_bytes=48 * 2**20
+        ),
+    )(block, near, far)
 
 
 def per_device(
@@ -73,7 +300,11 @@
     pair_cols = key_weight_matrix.shape[1]
     all_rows = tokens.shape[0] * head_count
     half_rows = all_rows // width_count
-    whole_rows = lax.all_gather(normed_inputs, "heads", axis=0, tiled=True)
+    own_kernels = head_count == RING_SIZE and width_count == 2
+    if own_kernels:
+        whole_rows = gather_rows(normed_inputs, 4, 1)
+    else:
+        whole_rows = lax.all_gather(normed_inputs, "heads", axis=0, tiled=True)
     swap = [(i, (i + 1) % width_count) for i in range(width_count)]
     other_rows = lax.ppermute(w_out, "width", swap)
     pair_sum = lax.psum_scatter(
@@ -88,7 +319,10 @@
         scatter_dimension=0,
         tiled=True,
     ).astype(jnp.bfloat16)
-    pair_rows = lax.all_gather(pair_sum, "heads", axis=0, tiled=False)
+    if own_kernels:
+        pair_rows = gather_rows(pair_sum, 1, 2)
+    else:
+        pair_rows = lax.all_gather(pair_sum, "heads", axis=0, tiled=False)
     pair_rows = pair_rows.reshape(head_count, half_rows, 2, pair_cols)
     projected_key_rows = jnp.swapaxes(pair_rows[:, :, 0], 0, 1).reshape(half_rows, -1)
     projected_value_rows = jnp.swapaxes(pair_rows[:, :, 1], 0, 1).reshape(half_rows, -1)
@@ -149,6 +383,8 @@
         "bngqk,bknd->bqngd", probabilities, value_heads, preferred_element_type=jnp.float32
     )
     attended = mixture.astype(jnp.bfloat16).reshape(half_rows, query_cols)
+    if own_kernels:
+        return gather_and_project(attended, w_out, other_rows, 4, 3)
     every_head = lax.all_gather(attended, "heads", axis=1, tiled=True)
     share = w_out.shape[0]
     own_part = lax.dynamic_slice_in_dim(every_head, width_index * share, share, 1)

time: 332 us -> 263 us (0.79)
  waiting for transfers between devices: 198 us -> 0.08 us
  Pallas kernels: 0 us -> 161 us
  matrix products: 63.3 us -> 27.9 us
  blocking collectives: 34.9 us -> 38.8 us
    all_gather x2 -> x0, waiting for transfers between devices: 198 us -> none  [the longest x1 101 us: per_device(): whole_rows = lax.all_gather(normed_inputs, 'heads', axis=0, tiled=True)]
    pallas_call x0 -> x3, Pallas kernels: none -> 161 us  [the longest x2 89 us: gather_rows(): pl.pallas_call(functools.partial(gather_kernel, chunks), out_shape=jax.Sh...]
    psum x1, blocking collectives: 2.59 us -> 38.8 us  [per_device(): square_sums = lax.psum(jnp.sum(widened * widened, axis=1), 'width')]
    all_gather x1 -> x0, blocking collectives: 32.3 us -> none  [per_device(): pair_rows = lax.all_gather(pair_sum, 'heads', axis=0, tiled=False)]
    dot_general x2 -> x0, matrix products: 32.1 us -> none  [the longest x1 16.2 us: per_device(): jnp.dot(own_part, w_out, preferred_element_type=jnp.float32)]
  transfers between devices with their start and end apart: 5 -> 3, of which waited for: 2 -> 0; matrix products, arithmetic and copies ran while one was open for 19% -> 17% of each run, Pallas kernels for 0% -> 34%
where the time goes in v2:
time: 263 us; the launch traced here: 262 us
  Pallas kernels  161 us (61%)
  blocking collectives  38.8 us (15%)
  matrix products  27.9 us (11%)
  between operations  13.7 us (5%)
  local copies, waits for them, and re-layouts  11.5 us (4%)
  other arithmetic  9.27 us (4%)
    pallas_call x2, Pallas kernels, gather_rows(): pl.pallas_call(functools.partial(gather_kernel, chunks), out_shape=jax.Sh...  89 us
    pallas_call x1, Pallas kernels, gather_and_project(): pl.pallas_call(functools.partial(project_kernel, chunks), out_shape=jax.S...  71.7 us
    psum x1, blocking collectives, per_device(): square_sums = lax.psum(jnp.sum(widened * widened, axis=1), 'width')  38.8 us
    dot_general x1, matrix products, per_device(): jnp.dot(whole_rows, w_query, preferred_element_type=jnp.float32)  22.2 us
  transfers between devices with their start and end apart: 3, of which 0 were waited for; matrix products, arithmetic and copies ran while one was open for 17% of the time, Pallas kernels for 34%

profile of v2, /device:TPU:0, one launch (start us, length us, event | category | flops | bytes accessed | tf_op | source)
XLA Modules:
  0.0 262.4 jit_solution(10617011340105595767)
XLA Ops:
  6.5 0.0 copy-start
  6.5 0.5 collective-permute-start
  7.0 0.9 convert_element_type.46
  7.9 1.4 fusion.2
  9.3 38.8 %psum.7 = f32[48]{0:T(128)S(1)} all-reduce(f32[48]{0:T(128)S(1)} %fusion.2), channel_id=1, replica_groups=mesh['groups'=2,'heads'=8,'width'=2] {'width'}, use_global_device_ids=true, to_apply=%region_1.0 | all-reduce | flops 48 | bytes 384 | tf_op jit(solution)/shard_map/psum | solution.py:293
  48.0 1.4 fusion.4.own_ref
  49.4 72.3 %shard_map.82 = bf16[384,8192]{1,0:T(8,128)(2,1)S(1)} custom-call(bf16[48,8192]{1,0:T(8,128)(2,1)S(1)} %fusion.4.own_ref), custom_call_target="tpu_custom_call" | custom-call | tf_op jit(solution)/shard_map/pallas_call | solution.py:174
  121.7 0.0 copy-start.3
  121.7 1.8 fusion.37
  123.5 1.0 copy-done.2
  124.6 0.3 copy-done.3
  124.9 1.8 fusion.36
  126.7 0.8 pad_maximum_fusion
  127.5 0.0 reduce-scatter.3.cloned.1.call-update
  127.5 0.0 reduce-scatter.5.cloned.1.call-start
  127.6 22.2 %fusion.38 = f32[384,2048]{1,0:T(8,128)} fusion(bf16[384,8192]{1,0:T(8,128)(2,1)} %copy-done.2, bf16[8192,2048]{1,0:T(8,128)(2,1)} %param.10), kind=kOutput, calls=%fused_computation.57 | convolution fusion | flops 12884901888 | bytes 42991616 | tf_op jit(solution)/shard_map/dot_general | solution.py:330
  149.7 0.0 reduce-scatter.5.cloned.1.call-update
  149.8 0.6 copy-done.4
  150.4 0.6 dynamic_slice.9
  151.0 0.6 dynamic_slice.8
  151.6 1.2 iota_compare_fusion.1
  152.8 0.1 fusion.21
  152.9 0.4 fusion.23
  153.3 0.0 reduce-scatter.3.cloned.1.call-done
  153.4 0.9 convert_element_type.48.own_ref
  154.3 16.7 %shard_map.83 = bf16[1536,256]{1,0:T(8,128)(2,1)S(1)} custom-call(bf16[192,256]{1,0:T(8,128)(2,1)S(1)} %convert_element_type.48.own_ref), custom_call_target="tpu_custom_call" | custom-call | tf_op jit(solution)/shard_map/pallas_call | solution.py:174
  171.0 0.2 reshape.260
  171.2 1.4 fusion.35
  172.6 1.2 copy.36
  173.8 1.2 copy.35
  175.1 0.3 constant_dynamic-slice_fusion
  175.3 0.1 copy.32
  175.5 0.1 copy.19
  175.6 0.4 fusion.29
  176.1 0.0 reduce-scatter.5.cloned.1.call-done
  176.1 1.7 copy.37
  177.8 0.5 fusion.34
  178.3 1.0 fusion.14
  179.3 1.0 fusion.1
  180.4 0.7 fusion
  181.1 1.1 fusion.11
  182.2 0.5 copy.26
  182.7 0.2 copy.52
  183.0 0.0 collective-permute-done.far_ref
  183.0 0.0 copy-start.1
  183.0 71.7 %shard_map.84 = bf16[192,2048]{1,0:T(8,128)(2,1)S(1)} custom-call(bf16[192,2048]{1,0:T(8,128)(2,1)S(1)} %bitcast.78, bf16[8192,2048]{1,0:T(8,128)(2,1)} %near_ref.1, bf16[8192,2048]{1,0:T(8,128)(2,1)} %collective-permute-done.far_ref), custom_call_target="tpu_custom_call" | custom-call | tf_op jit(solution)/shard_map/pallas_call | solution.py:255
  254.7 0.9 copy.54
  255.6 0.0 copy-done.1
  (9 shorter events, 0.1 us)
Async XLA Ops:
  6.5 115.2 %copy-start = (bf16[8192,128]{1,0:T(8,128)(2,1)S(1)}, bf16[8192,128]{1,0:T(8,128)(2,1)}, u32[]{:S(2)}) copy-start(bf16[8192,128]{1,0:T(8,128)(2,1)} %param.12) | copy-start | bytes 6291460
  6.5 146.8 %reduce-scatter.3.cloned.1.call-start = ((), (), s32[]{:S(2)}) async-start(), calls=%async_computation.2 | async-start | bytes 589824 | tf_op jit(solution)/shard_map/reduce_scatter | solution.py:310
  6.5 176.4 %collective-permute-start = (bf16[8192,2048]{1,0:T(8,128)(2,1)}, bf16[8192,2048]{1,0:T(8,128)(2,1)}, u32[]{:S(2)}, u32[]{:S(2)}) collective-permute-start(bf16[8192,2048]{1,0:T(8,128)(2,1)} %near_ref.1), channel_id=1, source_target_pairs={{0,1},{1,0},{2,3},{3,2},{4,5},{5,4},{6,7},{7,6},{8,9},{9,8},{10,11... | collective-permute-start | bytes 100663304 | tf_op jit(solution)/shard_map/ppermute | solution.py:309
  121.7 2.9 %copy-start.2 = (bf16[384,8192]{1,0:T(8,128)(2,1)}, bf16[384,8192]{1,0:T(8,128)(2,1)S(1)}, u32[]{:S(2)}) copy-start(bf16[384,8192]{1,0:T(8,128)(2,1)S(1)} %shard_map.82) | copy-start | bytes 18874372
  121.7 3.2 %copy-start.3 = (bf16[8192,128]{1,0:T(8,128)(2,1)S(1)}, bf16[8192,128]{1,0:T(8,128)(2,1)}, u32[]{:S(2)}) copy-start(bf16[8192,128]{1,0:T(8,128)(2,1)} %param.11) | copy-start | bytes 6291460
  127.5 48.6 %reduce-scatter.5.cloned.1.call-start = ((), (), s32[]{:S(2)}) async-start(), calls=%async_computation.3 | async-start | bytes 4718592 | tf_op jit(solution)/shard_map/reduce_scatter | solution.py:329
  149.7 0.7 copy-start.4
  149.7 1.2 copy-start.5
  183.0 72.6 %copy-start.1 = (bf16[8192,128]{1,0:T(8,128)(2,1)S(1)}, bf16[8192,128]{1,0:T(8,128)(2,1)}, u32[]{:S(2)}) copy-start(bf16[8192,128]{1,0:T(8,128)(2,1)} %param.12) | copy-start | bytes 6291460
Sparse Core Ops, SparseCore 0:
  127.6 7.9 reduce-scatter.2
  149.9 11.0 reduce-scatter.4

commit v3 on v2

--- a/solution.py
+++ b/solution.py
@@ -291,6 +291,9 @@
     width_index = lax.axis_index("width")
     widened = tokens.astype(jnp.float32)
     square_sums = lax.psum(jnp.sum(widened * widened, axis=1), "width")
+    square_sums, late_rows = lax.optimization_barrier((square_sums, w_out))
+    swap = [(i, (i + 1) % width_count) for i in range(width_count)]
+    other_rows = lax.ppermute(late_rows, "width", swap)
     normed_inputs = (
         widened
         * lax.rsqrt(square_sums[:, None] / MODEL_WIDTH + 1e-05)
@@ -302,11 +305,9 @@
     half_rows = all_rows // width_count
     own_kernels = head_count == RING_SIZE and width_count == 2
     if own_kernels:
-        whole_rows = gather_rows(normed_inputs, 4, 1)
+        whole_rows = gather_rows(normed_inputs, 8, 1)
     else:
         whole_rows = lax.all_gather(normed_inputs, "heads", axis=0, tiled=True)
-    swap = [(i, (i + 1) % width_count) for i in range(width_count)]
-    other_rows = lax.ppermute(w_out, "width", swap)
     pair_sum = lax.psum_scatter(
         jnp.concatenate(
             [
@@ -384,7 +385,7 @@
     )
     attended = mixture.astype(jnp.bfloat16).reshape(half_rows, query_cols)
     if own_kernels:
-        return gather_and_project(attended, w_out, other_rows, 4, 3)
+        return gather_and_project(attended, w_out, other_rows, 8, 3)
     every_head = lax.all_gather(attended, "heads", axis=1, tiled=True)
     share = w_out.shape[0]
     own_part = lax.dynamic_slice_in_dim(every_head, width_index * share, share, 1)

time: 263 us -> 229 us (0.87)
  blocking collectives: 38.8 us -> 2.59 us
    psum x1, blocking collectives: 38.8 us -> 2.59 us  [per_device(): square_sums = lax.psum(jnp.sum(widened * widened, axis=1), 'width')]
  transfers between devices with their start and end apart: 3 -> 3, of which waited for: 0 -> 0; matrix products, arithmetic and copies ran while one was open for 17% -> 19% of each run, Pallas kernels for 34% -> 40%
where the time goes in v3:
time: 229 us
  Pallas kernels  163 us (71%)
  matrix products  27.9 us (12%)
  between operations  13.7 us (6%)
  local copies, waits for them, and re-layouts  11.5 us (5%)
  other arithmetic  9.24 us (4%)
  blocking collectives  2.59 us (1%)
    pallas_call x2, Pallas kernels, gather_rows(): pl.pallas_call(functools.partial(gather_kernel, chunks), out_shape=jax.Sh...  90.9 us
    pallas_call x1, Pallas kernels, gather_and_project(): pl.pallas_call(functools.partial(project_kernel, chunks), out_shape=jax.S...  72.4 us
    dot_general x1, matrix products, per_device(): jnp.dot(whole_rows, w_query, preferred_element_type=jnp.float32)  22.2 us
    unnamed x16, local copies, waits for them, and re-layouts  4.89 us
  transfers between devices with their start and end apart: 3, of which 0 were waited for; matrix products, arithmetic and copies ran while one was open for 19% of the time, Pallas kernels for 40%

profile of v3, /device:TPU:0, one launch (start us, length us, event | category | flops | bytes accessed | tf_op | source)
XLA Modules:
  0.0 228.8 jit_solution(5760541357024201299)
XLA Ops:
  6.5 1.5 fusion.2
  8.1 2.6 %psum.7 = f32[48]{0:T(128)S(1)} all-reduce(f32[48]{0:T(128)S(1)} %fusion.2), channel_id=1, replica_groups=mesh['groups'=2,'heads'=8,'width'=2] {'width'}, use_global_device_ids=true, to_apply=%region_1.0 | all-reduce | flops 48 | bytes 384 | tf_op jit(solution)/shard_map/psum | solution.py:293
  10.7 0.3 collective-permute-start
  11.0 0.7 convert_element_type.46
  11.7 1.4 fusion.4.own_ref
  13.1 74.2 %shard_map.82 = bf16[384,8192]{1,0:T(8,128)(2,1)S(1)} custom-call(bf16[48,8192]{1,0:T(8,128)(2,1)S(1)} %fusion.4.own_ref), custom_call_target="tpu_custom_call" | custom-call | tf_op jit(solution)/shard_map/pallas_call | solution.py:174
  87.3 0.0 copy-done
  87.3 0.0 copy-start.2
  87.3 0.0 copy-start.3
  87.4 1.8 fusion.37
  89.1 1.0 copy-done.2
  90.2 0.3 copy-done.3
  90.5 1.8 fusion.36
  92.3 0.8 pad_maximum_fusion
  93.1 0.0 reduce-scatter.3.cloned.1.call-update
  93.1 0.0 reduce-scatter.5.cloned.1.call-start
  93.2 22.2 %fusion.38 = f32[384,2048]{1,0:T(8,128)} fusion(bf16[384,8192]{1,0:T(8,128)(2,1)} %copy-done.2, bf16[8192,2048]{1,0:T(8,128)(2,1)} %param.10), kind=kOutput, calls=%fused_computation.57 | convolution fusion | flops 12884901888 | bytes 42991616 | tf_op jit(solution)/shard_map/dot_general | solution.py:331
  115.4 0.0 reduce-scatter.5.cloned.1.call-update
  115.4 0.6 copy-done.4
  116.0 0.6 dynamic_slice.9
  116.6 0.6 dynamic_slice.8
  117.2 1.2 iota_compare_fusion.1
  118.4 0.1 fusion.21
  118.6 0.4 fusion.23
  118.9 0.0 reduce-scatter.3.cloned.1.call-done
  119.0 0.9 convert_element_type.48.own_ref
  119.9 16.7 %shard_map.83 = bf16[1536,256]{1,0:T(8,128)(2,1)S(1)} custom-call(bf16[192,256]{1,0:T(8,128)(2,1)S(1)} %convert_element_type.48.own_ref), custom_call_target="tpu_custom_call" | custom-call | tf_op jit(solution)/shard_map/pallas_call | solution.py:174
  136.6 0.2 reshape.260
  136.8 1.4 fusion.35
  138.2 1.2 copy.36
  139.5 1.2 copy.35
  140.7 0.3 constant_dynamic-slice_fusion
  141.0 0.1 copy.32
  141.1 0.1 copy.19
  141.3 0.4 fusion.29
  141.7 0.0 reduce-scatter.5.cloned.1.call-done
  141.7 1.7 copy.37
  143.4 0.5 fusion.34
  143.9 1.0 fusion.14
  144.9 1.0 fusion.1
  146.0 0.7 fusion
  146.7 1.1 fusion.11
  147.9 0.5 copy.26
  148.4 0.2 copy.52
  148.6 0.0 collective-permute-done.far_ref
  148.6 0.0 copy-start.1
  148.6 72.4 %shard_map.84 = bf16[192,2048]{1,0:T(8,128)(2,1)S(1)} custom-call(bf16[192,2048]{1,0:T(8,128)(2,1)S(1)} %bitcast.78, bf16[8192,2048]{1,0:T(8,128)(2,1)} %near_ref.1, bf16[8192,2048]{1,0:T(8,128)(2,1)} %collective-permute-done.far_ref), custom_call_target="tpu_custom_call" | custom-call | tf_op jit(solution)/shard_map/pallas_call | solution.py:255
  221.0 0.9 copy.54
  (9 shorter events, 0.1 us)
Async XLA Ops:
  6.5 80.8 %copy-start = (bf16[8192,128]{1,0:T(8,128)(2,1)S(1)}, bf16[8192,128]{1,0:T(8,128)(2,1)}, u32[]{:S(2)}) copy-start(bf16[8192,128]{1,0:T(8,128)(2,1)} %param.12) | copy-start | bytes 6291460
  6.5 112.4 %reduce-scatter.3.cloned.1.call-start = ((), (), s32[]{:S(2)}) async-start(), calls=%async_computation.2 | async-start | bytes 589824 | tf_op jit(solution)/shard_map/reduce_scatter | solution.py:311
  10.7 137.9 %collective-permute-start = (bf16[8192,2048]{1,0:T(8,128)(2,1)}, bf16[8192,2048]{1,0:T(8,128)(2,1)}, u32[]{:S(2)}, u32[]{:S(2)}) collective-permute-start(bf16[8192,2048]{1,0:T(8,128)(2,1)} %near_ref.1), channel_id=1, source_target_pairs={{0,1},{1,0},{2,3},{3,2},{4,5},{5,4},{6,7},{7,6},{8,9},{9,8},{10,11... | collective-permute-start | bytes 100663304 | tf_op jit(solution)/shard_map/ppermute | solution.py:296
  87.3 2.9 %copy-start.2 = (bf16[384,8192]{1,0:T(8,128)(2,1)}, bf16[384,8192]{1,0:T(8,128)(2,1)S(1)}, u32[]{:S(2)}) copy-start(bf16[384,8192]{1,0:T(8,128)(2,1)S(1)} %shard_map.82) | copy-start | bytes 18874372
  87.3 3.2 %copy-start.3 = (bf16[8192,128]{1,0:T(8,128)(2,1)S(1)}, bf16[8192,128]{1,0:T(8,128)(2,1)}, u32[]{:S(2)}) copy-start(bf16[8192,128]{1,0:T(8,128)(2,1)} %param.11) | copy-start | bytes 6291460
  93.1 48.6 %reduce-scatter.5.cloned.1.call-start = ((), (), s32[]{:S(2)}) async-start(), calls=%async_computation.3 | async-start | bytes 4718592 | tf_op jit(solution)/shard_map/reduce_scatter | solution.py:330
  115.3 0.7 copy-start.4
  115.3 1.2 copy-start.5
  148.6 73.3 %copy-start.1 = (bf16[8192,128]{1,0:T(8,128)(2,1)S(1)}, bf16[8192,128]{1,0:T(8,128)(2,1)}, u32[]{:S(2)}) copy-start(bf16[8192,128]{1,0:T(8,128)(2,1)} %param.12) | copy-start | bytes 6291460
Sparse Core Ops, SparseCore 0:
  93.2 7.9 reduce-scatter.2
  115.5 11.0 reduce-scatter.4

commit v4 on v3

--- a/solution.py
+++ b/solution.py
@@ -185,6 +185,57 @@
             collective_id=collective_id, has_side_effects=True, vmem_limit_bytes=24 * 2**20
         ),
     )(block)
+
+
+def trade_kernel(give_ref, take_ref, own_sem, send_sem, recv_sem):
+    me = lax.axis_index("heads")
+    barrier = pltpu.get_barrier_semaphore()
+    keep = pltpu.make_async_copy(give_ref.at[me], take_ref.at[me], own_sem)
+    keep.start()
+    for offset in range(1, RING_SIZE):
+        pl.semaphore_signal(
+            barrier,
+            inc=1,
+            device_id={"heads": (me + offset) % RING_SIZE},
+            device_id_type=pl.DeviceIdType.MESH,
+        )
+    pl.semaphore_wait(barrier, RING_SIZE - 1)
+
+    def trade(offset, source_ref, target_ref):
+        return pltpu.make_async_remote_copy(
+            src_ref=source_ref,
+            dst_ref=target_ref,
+            send_sem=send_sem.at[offset - 1],
+            recv_sem=recv_sem.at[offset - 1],
+            device_id={"heads": (me + offset) % RING_SIZE},
+            device_id_type=pl.DeviceIdType.MESH,
+        )
+
+    for offset in range(1, RING_SIZE):
+        peer = (me + offset) % RING_SIZE
+        trade(offset, give_ref.at[peer], take_ref.at[me]).start()
+    keep.wait()
+    for offset in range(1, RING_SIZE):
+        source = (me + RING_SIZE - offset) % RING_SIZE
+        trade(offset, give_ref.at[source], take_ref.at[source]).wait_recv()
+    for offset in range(1, RING_SIZE):
+        peer = (me + offset) % RING_SIZE
+        trade(offset, give_ref.at[peer], take_ref.at[me]).wait_send()
+
+
+def trade_blocks(blocks, collective_id):
+    return pl.pallas_call(
+        trade_kernel,
+        out_shape=jax.ShapeDtypeStruct(blocks.shape, blocks.dtype),
+        in_specs=[pl.BlockSpec(memory_space=pltpu.VMEM)],
+        out_specs=pl.BlockSpec(memory_space=pltpu.VMEM),
+        scratch_shapes=[
+            pltpu.SemaphoreType.DMA,
+            pltpu.SemaphoreType.DMA((RING_SIZE - 1,)),
+            pltpu.SemaphoreType.DMA((RING_SIZE - 1,)),
+        ],
+        compiler_params=pltpu.CompilerParams(collective_id=collective_id, has_side_effects=True),
+    )(blocks)
 
 
 WEIGHT_SLOTS = 3
@@ -321,12 +372,15 @@
         tiled=True,
     ).astype(jnp.bfloat16)
     if own_kernels:
-        pair_rows = gather_rows(pair_sum, 1, 2)
+        piece = pair_cols // KEY_VALUE_HEADS
+        blocks = pair_sum.reshape(half_rows, 2 * piece, KEY_VALUE_HEADS).transpose(2, 1, 0)
+        traded = trade_blocks(blocks, 2).reshape(head_count, 2, piece, half_rows)
+        traded = traded.transpose(1, 3, 0, 2).reshape(2, -1, PROMPT_SLOTS, 1, HEAD_WIDTH)
     else:
         pair_rows = lax.all_gather(pair_sum, "heads", axis=0, tiled=False)
-    pair_rows = pair_rows.reshape(head_count, half_rows, 2, pair_cols)
-    projected_key_rows = jnp.swapaxes(pair_rows[:, :, 0], 0, 1).reshape(half_rows, -1)
-    projected_value_rows = jnp.swapaxes(pair_rows[:, :, 1], 0, 1).reshape(half_rows, -1)
+        pair_rows = pair_rows.reshape(head_count, half_rows, 2, pair_cols)
+        projected_key_rows = jnp.swapaxes(pair_rows[:, :, 0], 0, 1).reshape(half_rows, -1)
+        projected_value_rows = jnp.swapaxes(pair_rows[:, :, 1], 0, 1).reshape(half_rows, -1)
     query_sum = lax.psum_scatter(
         jnp.dot(whole_rows, w_query, preferred_element_type=jnp.float32),
         "width",
@@ -344,21 +398,24 @@
         cosine_table,
         sine_table,
     ).astype(jnp.bfloat16)
-    key_grid = jnp.swapaxes(
-        projected_key_rows.reshape(prompts_in_group, PROMPT_SLOTS, HEAD_WIDTH, KEY_VALUE_HEADS),
-        2,
-        3,
-    )
-    value_grid = jnp.swapaxes(
-        projected_value_rows.reshape(prompts_in_group, PROMPT_SLOTS, HEAD_WIDTH, KEY_VALUE_HEADS),
-        2,
-        3,
-    )
-    key_heads = lax.dynamic_slice_in_dim(key_grid, leading_shared_slot, heads_sharing_key, 2)
+    if own_kernels:
+        key_heads, value_heads = traded[0], traded[1]
+    else:
+        key_grid = jnp.swapaxes(
+            projected_key_rows.reshape(prompts_in_group, PROMPT_SLOTS, HEAD_WIDTH, KEY_VALUE_HEADS),
+            2,
+            3,
+        )
+        value_grid = jnp.swapaxes(
+            projected_value_rows.reshape(prompts_in_group, PROMPT_SLOTS, HEAD_WIDTH, KEY_VALUE_HEADS),
+            2,
+            3,
+        )
+        key_heads = lax.dynamic_slice_in_dim(key_grid, leading_shared_slot, heads_sharing_key, 2)
+        value_heads = lax.dynamic_slice_in_dim(value_grid, leading_shared_slot, heads_sharing_key, 2)
     rotated_keys = rotate(key_heads.astype(jnp.float32), cosine_table, sine_table).astype(
         jnp.bfloat16
     )
-    value_heads = lax.dynamic_slice_in_dim(value_grid, leading_shared_slot, heads_sharing_key, 2)
     lengths_here = lax.dynamic_slice_in_dim(
         prompt_len, width_index * prompts_in_group, prompts_in_group
     )

time: 229 us -> 220 us (0.961)
  Pallas kernels: 163 us -> 156 us
    pallas_call x2 -> x1, Pallas kernels: 90.9 us -> 74.2 us  [gather_rows(): pl.pallas_call(functools.partial(gather_kernel, chunks), out_shape=jax.Sh...]
    pallas_call x0 -> x1, Pallas kernels: none -> 8.41 us  [trade_blocks(): pl.pallas_call(trade_kernel, out_shape=jax.ShapeDtypeStruct(blocks.shape,...]
    transpose x2 -> x0, local copies, waits for them, and re-layouts: 2.44 us -> none  [the longest x1 1.22 us: per_device(): jnp.swapaxes(pair_rows[:, :, 0], 0, 1).reshape(half_rows, -1)]
    unnamed x16 -> x19, local copies, waits for them, and re-layouts: 4.89 us -> 6.76 us
  transfers between devices with their start and end apart: 3 -> 3, of which waited for: 0 -> 0; matrix products, arithmetic and copies ran while one was open for 19% -> 19% of each run, Pallas kernels for 40% -> 38%
where the time goes in v4:
time: 220 us; the launch traced here: 219 us
  Pallas kernels  156 us (71%)
  matrix products  28.1 us (13%)
  between operations  13.6 us (6%)
  local copies, waits for them, and re-layouts  10.6 us (5%)
  other arithmetic  7.55 us (3%)
  blocking collectives  2.59 us (1%)
    pallas_call x1, Pallas kernels, gather_rows(): pl.pallas_call(functools.partial(gather_kernel, chunks), out_shape=jax.Sh...  74.2 us
    pallas_call x1, Pallas kernels, gather_and_project(): pl.pallas_call(functools.partial(project_kernel, chunks), out_shape=jax.S...  73.5 us
    dot_general x1, matrix products, per_device(): jnp.dot(whole_rows, w_query, preferred_element_type=jnp.float32)  22.2 us
    pallas_call x1, Pallas kernels, trade_blocks(): pl.pallas_call(trade_kernel, out_shape=jax.ShapeDtypeStruct(blocks.shape,...  8.41 us
    unnamed x19, local copies, waits for them, and re-layouts  6.76 us
  transfers between devices with their start and end apart: 3, of which 0 were waited for; matrix products, arithmetic and copies ran while one was open for 19% of the time, Pallas kernels for 38%

profile of v4, /device:TPU:0, one launch (start us, length us, event | category | flops | bytes accessed | tf_op | source)
XLA Modules:
  0.0 219.2 jit_solution(16887035912620063368)
XLA Ops:
  6.5 0.0 copy-start
  6.5 0.0 reduce-scatter.7.cloned.1.call-start
  6.5 1.5 fusion.2
  8.1 2.6 %psum.7 = f32[48]{0:T(128)S(1)} all-reduce(f32[48]{0:T(128)S(1)} %fusion.2), channel_id=1, replica_groups=mesh['groups'=2,'heads'=8,'width'=2] {'width'}, use_global_device_ids=true, to_apply=%region_1.0 | all-reduce | flops 48 | bytes 384 | tf_op jit(solution)/shard_map/psum | solution.py:344
  10.7 0.3 collective-permute-start
  11.0 0.7 convert_element_type.48
  11.7 1.4 fusion.4.own_ref
  13.1 74.2 %shard_map.82 = bf16[384,8192]{1,0:T(8,128)(2,1)S(1)} custom-call(bf16[48,8192]{1,0:T(8,128)(2,1)S(1)} %fusion.4.own_ref), custom_call_target="tpu_custom_call" | custom-call | tf_op jit(solution)/shard_map/pallas_call | solution.py:174
  87.3 0.0 copy-done
  87.3 0.0 copy-start.2
  87.3 0.0 copy-start.3
  87.4 1.9 fusion.37
  89.3 0.9 copy-done.2
  90.2 0.3 copy-done.3
  90.5 1.9 fusion.36
  92.4 0.9 copy.36
  93.3 0.0 reduce-scatter.7.cloned.1.call-update
  93.3 0.2 reduce-scatter.5.cloned.1.call-start
  93.6 22.2 %fusion.38 = f32[384,2048]{1,0:T(8,128)} fusion(bf16[384,8192]{1,0:T(8,128)(2,1)} %copy-done.2, bf16[8192,2048]{1,0:T(8,128)(2,1)} %param.10), kind=kOutput, calls=%fused_computation.58 | convolution fusion | flops 12884901888 | bytes 42991616 | tf_op jit(solution)/shard_map/dot_general | solution.py:385
  115.8 0.0 reduce-scatter.5.cloned.1.call-update
  115.8 0.6 copy-done.4
  116.4 0.6 dynamic_slice.7
  117.0 0.0 copy-done.5
  117.0 0.6 dynamic_slice.6
  117.6 1.2 iota_compare_fusion.1
  118.9 0.1 fusion.21
  119.0 0.4 fusion.23
  119.4 0.0 reduce-scatter.7.cloned.1.call-done
  119.4 1.0 copy.37
  120.4 0.7 copy.61
  121.1 8.4 %shard_map.83 = bf16[8,32,192]{2,1,0:T(8,128)(2,1)} custom-call(bf16[8,32,192]{2,1,0:T(8,128)(2,1)} %bitcast.83), custom_call_target="tpu_custom_call" | custom-call | tf_op jit(solution)/shard_map/pallas_call | solution.py:227
  129.5 0.9 copy.60
  130.5 0.1 copy.39
  130.6 0.1 copy.38
  130.7 0.4 fusion.26
  131.1 0.0 reduce-scatter.5.cloned.1.call-done
  131.1 1.7 copy.42
  132.8 0.5 fusion.33
  133.3 1.0 fusion.14
  134.4 1.0 fusion.1
  135.4 0.7 fusion
  136.1 1.1 fusion.11
  137.3 0.5 copy.32
  137.8 0.2 copy.59
  138.0 0.0 collective-permute-done.far_ref
  138.0 0.0 copy-start.1
  138.0 73.5 %shard_map.84 = bf16[192,2048]{1,0:T(8,128)(2,1)S(1)} custom-call(bf16[192,2048]{1,0:T(8,128)(2,1)S(1)} %bitcast.77, bf16[8192,2048]{1,0:T(8,128)(2,1)} %near_ref.1, bf16[8192,2048]{1,0:T(8,128)(2,1)} %collective-permute-done.far_ref), custom_call_target="tpu_custom_call" | custom-call | tf_op jit(solution)/shard_map/pallas_call | solution.py:306
  211.5 0.9 copy.63
  (9 shorter events, 0.1 us)
Async XLA Ops:
  6.5 80.8 %copy-start = (bf16[8192,128]{1,0:T(8,128)(2,1)S(1)}, bf16[8192,128]{1,0:T(8,128)(2,1)}, u32[]{:S(2)}) copy-start(bf16[8192,128]{1,0:T(8,128)(2,1)} %param.12) | copy-start | bytes 6291460
  6.5 112.8 %reduce-scatter.7.cloned.1.call-start = ((), (), s32[]{:S(2)}) async-start(), calls=%async_computation.3 | async-start | bytes 589824
  10.7 127.3 %collective-permute-start = (bf16[8192,2048]{1,0:T(8,128)(2,1)}, bf16[8192,2048]{1,0:T(8,128)(2,1)}, u32[]{:S(2)}, u32[]{:S(2)}) collective-permute-start(bf16[8192,2048]{1,0:T(8,128)(2,1)} %near_ref.1), channel_id=1, source_target_pairs={{0,1},{1,0},{2,3},{3,2},{4,5},{5,4},{6,7},{7,6},{8,9},{9,8},{10,11... | collective-permute-start | bytes 100663304 | tf_op jit(solution)/shard_map/ppermute | solution.py:347
  87.3 2.9 %copy-start.2 = (bf16[384,8192]{1,0:T(8,128)(2,1)}, bf16[384,8192]{1,0:T(8,128)(2,1)S(1)}, u32[]{:S(2)}) copy-start(bf16[384,8192]{1,0:T(8,128)(2,1)S(1)} %shard_map.82) | copy-start | bytes 18874372
  87.3 3.2 %copy-start.3 = (bf16[8192,128]{1,0:T(8,128)(2,1)S(1)}, bf16[8192,128]{1,0:T(8,128)(2,1)}, u32[]{:S(2)}) copy-start(bf16[8192,128]{1,0:T(8,128)(2,1)} %param.11) | copy-start | bytes 6291460
  93.3 37.8 %reduce-scatter.5.cloned.1.call-start = ((), (), s32[]{:S(2)}) async-start(), calls=%async_computation.2 | async-start | bytes 4718592 | tf_op jit(solution)/shard_map/reduce_scatter | solution.py:384
  115.8 0.7 copy-start.4
  115.8 1.2 copy-start.5
  138.0 74.4 %copy-start.1 = (bf16[8192,128]{1,0:T(8,128)(2,1)S(1)}, bf16[8192,128]{1,0:T(8,128)(2,1)}, u32[]{:S(2)}) copy-start(bf16[8192,128]{1,0:T(8,128)(2,1)} %param.12) | copy-start | bytes 6291460
Sparse Core Ops, SparseCore 0:
  93.5 7.9 reduce-scatter.6
  115.9 11.0 reduce-scatter.4
